TPU v7x, 128 devices: a whole 4x4x4 slice. The times are simulated.
128 devices in a mesh: gx: 4 (over y_lo, core), gy: 4 (over z), gz: 8 (over y_hi, x).
Axes of the slice: x: 4, y: 4 (y_hi: 2, y_lo: 2; y = y_hi * 2 + y_lo), z: 4, core: 2. Of those that a mesh axis runs over, the one named last changes fastest.
Arguments:
- right_sides: float32 [6, 128, 128, 1024], P(None, 'gx', 'gy', 'gz'), may hold values from -6 to 6
- permeability: float32 [128, 128, 1024], P('gx', 'gy', 'gz'), may hold values from 0.1 to 10
Outputs:
- basis_q: float32 [24, 128, 128, 1024], P(None, 'gx', 'gy', 'gz')
- factor_r: float32 [24, 24], replicated
All inputs are finite; a program needn't handle non-finite values.
Results may differ from a plain program's by a relative error of at most 0.00012.
Values sent between devices are 32-bit elements; how exact they have to be, the bound alone decides.
A program may use at most 128 MiB of HBM per device.

v0:
```python
import jax
import jax.numpy as jnp
from jax import lax
from jax.sharding import PartitionSpec as P


def extended(cells, sides, width):
    for axis, dim in sides:
        count = lax.axis_size(axis)
        ends = count - 1
        head = lax.slice_in_dim(cells, 0, width, axis=dim)
        tail = lax.slice_in_dim(cells, cells.shape[dim] - width, cells.shape[dim], axis=dim)
        cells = jnp.concatenate(
            [
                lax.ppermute(tail, axis, [(i, (i + 1) % count) for i in range(ends)]),
                cells,
                lax.ppermute(head, axis, [((i + 1) % count, i) for i in range(ends)]),
            ],
            axis=dim,
        )
    return cells


def face_weights(kappa_pad):
    center = kappa_pad[1:-1, 1:-1, 1:-1]
    others = [
        kappa_pad[2:, 1:-1, 1:-1],
        kappa_pad[:-2, 1:-1, 1:-1],
        kappa_pad[1:-1, 2:, 1:-1],
        kappa_pad[1:-1, :-2, 1:-1],
        kappa_pad[1:-1, 1:-1, 2:],
        kappa_pad[1:-1, 1:-1, :-2],
    ]
    face_list = []
    for neighbour in others:
        divisor = center + neighbour
        divisor = jnp.where(divisor > 0, divisor, 1.0)
        face_list.append(2.0 * center * neighbour / divisor)
    diagonal = face_list[0]
    for weight in face_list[1:]:
        diagonal = diagonal + weight
    diagonal = jnp.where(diagonal > 0, diagonal, 1.0)
    return (face_list, diagonal)


def stencil(field_pad, face_list, diagonal):
    slices = [
        field_pad[:, 2:, 1:-1, 1:-1],
        field_pad[:, :-2, 1:-1, 1:-1],
        field_pad[:, 1:-1, 2:, 1:-1],
        field_pad[:, 1:-1, :-2, 1:-1],
        field_pad[:, 1:-1, 1:-1, 2:],
        field_pad[:, 1:-1, 1:-1, :-2],
    ]
    accum = face_list[0] * slices[0]
    for weight, piece in zip(face_list[1:], slices[1:]):
        accum = accum + weight * piece
    return 2.5 * accum / diagonal


def lower_factor(matrix):
    order = matrix.shape[0]
    positions = jnp.arange(order)
    lower = jnp.zeros_like(matrix)
    for column in range(order):
        remain = matrix[:, column] - jnp.dot(lower, lower[column], precision=lax.Precision.HIGHEST)
        pivot = jnp.sqrt(remain[column])
        entries = jnp.where(
            positions > column, remain / pivot, jnp.where(positions == column, pivot, 0.0)
        )
        lower = lower + entries[:, None] * (positions[None, :] == column).astype(matrix.dtype)
    return lower


def lower_inverse(lower):
    order = lower.shape[0]
    positions = jnp.arange(order)
    inverse = jnp.zeros_like(lower)
    for row_index in range(order):
        unit_row = (positions == row_index).astype(lower.dtype)
        partial_row = unit_row - jnp.dot(lower[row_index], inverse, precision=lax.Precision.HIGHEST)
        new_row = partial_row / lower[row_index, row_index]
        inverse = inverse + unit_row[:, None] * new_row[None, :]
    return inverse


def on_device(right_sides, permeability):
    depth = 3
    powers = [right_sides]
    kappa_pad = extended(permeability, (("gx", 0), ("gy", 1), ("gz", 2)), 1)
    face_list, diagonal = face_weights(kappa_pad)
    field = right_sides
    for power_index in range(depth):
        padded = extended(field, (("gx", 1), ("gy", 2), ("gz", 3)), 1)
        field = stencil(padded, face_list, diagonal)
        powers.append(field)
    basis = jnp.concatenate(powers, 0)
    columns = basis.shape[0]
    flat = basis.reshape(columns, -1)
    cell_count = flat.shape[1] * lax.axis_size("gx") * lax.axis_size("gy") * lax.axis_size("gz")
    gram = jnp.dot(flat, flat.T, precision=lax.Precision.HIGHEST)
    total_gram = lax.psum(gram, ("gx", "gy", "gz"))
    factor_r = lower_factor(total_gram / cell_count).T
    inverse = lower_inverse(factor_r.T)
    solved = jnp.dot(inverse, flat, precision=lax.Precision.HIGHEST)
    return (solved.reshape(basis.shape), factor_r)


def solution(mesh):
    placed = (P(None, "gx", "gy", "gz"), P("gx", "gy", "gz"))
    return jax.shard_map(
        on_device,
        mesh=mesh,
        in_specs=placed,
        out_specs=(P(None, "gx", "gy", "gz"), P()),
        check_vma=False,
    )
```

profile of v0, /device:TPU:1, one launch (start us, length us, event | category | flops | bytes accessed | tf_op | source)
XLA Modules:
  0.0 477.7 jit_solution(12275474916651257987)
XLA Ops:
  1.4 4.6 collective-permute-start.2
  6.0 1.9 collective-permute-start
  8.0 4.7 copy.166
  12.6 2.1 copy-done.5
  15.4 3.8 collective-permute-start.3
  24.9 4.2 collective-permute-start.6
  35.6 4.0 collective-permute-start.10
  39.6 2.8 copy_dynamic-update-slice_fusion
  42.5 2.1 copy-done.6
  45.9 4.3 collective-permute-start.7
  53.3 2.7 pad_maximum_fusion.1
  56.0 5.2 %fusion.259 = (f32[6,34,34,1]{3,0,2,1:T(8,128)}, f32[6,34,34,1]{3,0,2,1:T(8,128)}) fusion(f32[6,34,34,128]{3,0,2,1:T(8,128)S(1)} %pad_maximum_fusion.1), kind=kLoop, calls=%fused_computation.574 | loop fusion | bytes 110976 | tf_op jit(solution)/shard_map/slice | solution.py:11
  61.2 3.9 copy.152
  66.5 3.9 copy.156
  70.4 4.8 collective-permute-start.11
  75.2 4.7 compare_select_fusion
  79.9 4.4 copy.153
  84.3 4.3 copy.157
  88.6 15.8 %fusion.31 = f32[6,32,32,128]{3,0,2,1:T(8,128)S(1)} fusion(f32[6,34,34,1]{3,0,2,1:T(8,128)} %copy.157, f32[6,34,1,128]{3,0,2,1:T(8,128)S(1)} %collective-permute-done.5, f32[6,34,32,128]{3,0,2,1:T(8,128)} %copy-done.6, f32[6,34,1,128]{3,0,2,1:T(8,128)S(1)} %collective-permute-done.7, f32[6,34,34,1]{3,0,2,1:T(8,128)} %copy.153, ...), kind=kLoop, calls=%fused_computation.73 | loop fusion | flops 18087936 | bytes 13764800 | tf_op jit(solution)/shard_map/div | solution.py:58
  104.5 3.2 collective-permute-start.12
  107.7 4.9 %collective-permute-start.13 = (f32[6,1,32,128]{3,0,2,1:T(8,128)S(1)}, f32[6,1,32,128]{3,0,2,1:T(8,128)S(1)}, u32[]{:S(2)}, u32[]{:S(2)}) collective-permute-start(f32[6,1,32,128]{3,0,2,1:T(8,128)S(1)} %get-tuple-element.59), channel_id=1, source_target_pairs={{0,32},{32,64},{64,96},{1,33},{33,65},{65,97},{2,34},{34,66},{66,9... | collective-permute-start | bytes 294920 | tf_op jit(solution)/shard_map/ppermute | solution.py:15
  115.8 4.3 collective-permute-start.15
  123.2 5.2 %fusion.258 = (f32[6,34,34,1]{3,0,2,1:T(8,128)}, f32[6,34,34,1]{3,0,2,1:T(8,128)}) fusion(f32[6,34,34,128]{3,0,2,1:T(8,128)S(1)} %pad_maximum_fusion.2), kind=kLoop, calls=%fused_computation.573 | loop fusion | bytes 110976 | tf_op jit(solution)/shard_map/slice | solution.py:11
  128.4 3.3 copy.158
  133.0 3.9 copy.160
  136.9 4.8 %collective-permute-start.17 = (f32[6,34,34,1]{2,3,1,0:T(1,128)}, f32[6,34,34,1]{2,3,1,0:T(1,128)}, u32[]{:S(2)}, u32[]{:S(2)}) collective-permute-start(f32[6,34,34,1]{2,3,1,0:T(1,128)} %copy.160), channel_id=1, source_target_pairs={{0,1},{1,2},{2,3},{3,4},{4,5},{5,6},{6,7},{8,9},{9,10},{10,11},{11... | collective-permute-start | bytes 83240 | tf_op jit(solution)/shard_map/ppermute | solution.py:15
  142.3 4.4 copy.159
  146.7 4.3 copy.161
  151.0 18.5 %fusion.18 = f32[6,32,32,128]{3,0,2,1:T(8,128)S(1)} fusion(f32[6,34,34,1]{3,0,2,1:T(8,128)} %copy.161, f32[6,34,1,128]{3,0,2,1:T(8,128)} %copy-done.14, f32[6,34,1,128]{3,0,2,1:T(8,128)} %copy-done.16, f32[6,1,32,128]{3,0,2,1:T(8,128)S(1)} %collective-permute-done.12, f32[6,32,32,128]{3,0,2,1:T(8,128)} %copy-done.1, ...), kind=kLoop, calls=%fused_computation.42 | loop fusion | flops 24379392 | bytes 10422464 | tf_op jit(solution)/shard_map/div | solution.py:58
  169.5 1.9 collective-permute-start.18
  171.4 5.8 %collective-permute-start.19 = (f32[6,1,32,128]{3,0,2,1:T(8,128)S(1)}, f32[6,1,32,128]{3,0,2,1:T(8,128)S(1)}, u32[]{:S(2)}, u32[]{:S(2)}) collective-permute-start(f32[6,1,32,128]{3,0,2,1:T(8,128)S(1)} %get-tuple-element.57), channel_id=1, source_target_pairs={{0,32},{32,64},{64,96},{1,33},{33,65},{65,97},{2,34},{34,66},{66,9... | collective-permute-start | bytes 294920 | tf_op jit(solution)/shard_map/ppermute | solution.py:15
  180.5 4.7 collective-permute-start.21
  188.3 5.2 %fusion.257 = (f32[6,34,34,1]{3,0,2,1:T(8,128)}, f32[6,34,34,1]{3,0,2,1:T(8,128)}) fusion(f32[6,34,34,128]{3,0,2,1:T(8,128)S(1)} %pad_maximum_fusion.3), kind=kLoop, calls=%fused_computation.572 | loop fusion | bytes 110976 | tf_op jit(solution)/shard_map/slice | solution.py:11
  193.5 3.3 copy.162
  198.1 3.3 copy.164
  201.4 4.8 %collective-permute-start.23 = (f32[6,34,34,1]{2,3,1,0:T(1,128)S(1)}, f32[6,34,34,1]{2,3,1,0:T(1,128)S(1)}, u32[]{:S(2)}, u32[]{:S(2)}) collective-permute-start(f32[6,34,34,1]{2,3,1,0:T(1,128)S(1)} %copy.164), channel_id=1, source_target_pairs={{0,1},{1,2},{2,3},{3,4},{4,5},{5,6},{6,7},{8,9},{9,10},{10,11},{11... | collective-permute-start | bytes 83240 | tf_op jit(solution)/shard_map/ppermute | solution.py:15
  206.8 3.6 copy.163
  210.4 3.5 copy.165
  213.9 19.3 %fusion.5 = f32[6,32,32,128]{3,0,2,1:T(8,128)} fusion(f32[6,34,34,1]{3,0,2,1:T(8,128)} %copy.165, f32[6,34,1,128]{3,0,2,1:T(8,128)} %copy-done.13, f32[6,34,1,128]{3,0,2,1:T(8,128)} %copy-done.15, f32[6,1,32,128]{3,0,2,1:T(8,128)} %copy-done.11, f32[6,32,32,128]{3,0,2,1:T(8,128)} %copy-done.3, f32[6,1,32,128]{3,0,2,1:T(8,128)} %copy-done.12, ...), kind=kLoop, calls=%fused_computation.11 | loop fusion | flops 24379392 | bytes 10422464 | tf_op jit(solution)/shard_map/div | solution.py:58
  233.2 6.2 %pad_maximum_fusion = f32[24,32,32,128]{3,0,2,1:T(8,128)S(1)} fusion(f32[6,32,32,128]{3,0,2,1:T(8,128)} %fusion.5, f32[6,32,32,128]{3,0,2,1:T(8,128)S(1)} %copy-done.4, f32[6,32,32,128]{3,0,2,1:T(8,128)S(1)} %copy-done.2, f32[6,32,32,128]{3,0,2,1:T(8,128)} %copy-done.5), kind=kLoop, calls=%fused_computation.1 | loop fusion | flops 9437184 | bytes 25165824 | tf_op jit(solution)/shard_map/concatenate | solution.py:97
  239.5 4.8 copy-done
  244.4 13.1 %convolution_bitcast_fusion = f32[24,24]{1,0:T(8,128)S(1)} fusion(f32[24,32,32,128]{3,0,2,1:T(8,128)S(1)} %pad_maximum_fusion), kind=kOutput, calls=%fused_computation.99 | convolution fusion | flops 905969664 | bytes 12585216 | tf_op jit(solution)/shard_map/dot_general | solution.py:101
  257.5 83.5 %psum.7 = f32[24,24]{1,0:T(8,128)S(1)} all-reduce(f32[24,24]{1,0:T(8,128)S(1)} %convolution_bitcast_fusion), channel_id=1, replica_groups=mesh['gx'=4,'gy'=4,'gz'=8] {'gx','gy','gz'}, use_global_device_ids=true, to_apply=%region_0.1 | all-reduce | flops 576 | bytes 4608 | tf_op jit(solution)/shard_map/psum | solution.py:102
  381.4 11.5 %copy.167 = f32[24,32,32,128]{3,2,1,0:T(8,128)} copy(f32[24,32,32,128]{3,0,2,1:T(8,128)} %copy-done) | data formatting | bytes 25165824 | tf_op jit(solution)/shard_map/concatenate | solution.py:97
  409.7 16.8 %copy.180 = f32[3,8,1024,128]{3,1,2,0:T(8,128)} copy(f32[3,8,1024,128]{3,2,1,0:T(8,128)} %bitcast.525) | data formatting | bytes 25165824
  426.5 11.3 %copy.175 = f32[3,8,1024,128]{3,2,1,0:T(8,128)} copy(f32[3,8,1024,128]{3,1,2,0:T(8,128)} %copy.180) | data formatting | bytes 25165824
  441.0 24.5 %fusion = f32[24,32,32,128]{3,0,2,1:T(8,128)} fusion(f32[32,32,128,24]{2,1,0,3:T(8,128)} %bitcast.526, f32[24,24]{1,0:T(8,128)S(1)} %multiply_add_fusion.5, f32[24]{0:T(128)S(1)} %fusion.112, f32[24]{0:T(128)S(1)} %copy-done.44, f32[24]{0:T(128)S(1)} %fusion.111, f32[24]{0:T(128)S(1)} %copy-done.43, f32[24]{0:T(128)S(1)} %fusion.110, f32[24]{0:T(128)S(1)} %copy-done.42, ...), kind=kOutput, calls=%fused_computation.2 | convolution fusion | flops 905974272 | bytes 25168896 | tf_op jit(solution)/shard_map/dot_general | solution.py:105
  465.5 11.8 %copy.169 = f32[24,32,32,128]{3,2,1,0:T(8,128)} copy(f32[24,32,32,128]{3,0,2,1:T(8,128)} %fusion) | data formatting | bytes 25165824
  (286 shorter events, 79.8 us)
Async XLA Ops:
  0.6 21.7 %copy-start.10 = (f32[32,32,128]{2,1,0:T(8,128)S(1)}, f32[32,32,128]{2,1,0:T(8,128)}, u32[]{:S(2)}) copy-start(f32[32,32,128]{2,1,0:T(8,128)} %param.3) | copy-start | bytes 1572868
  1.4 20.9 %collective-permute-start.2 = (f32[1,32,128]{2,1,0:T(8,128)S(1)}, f32[1,32,128]{2,1,0:T(8,128)S(1)}, u32[]{:S(2)}, u32[]{:S(2)}) collective-permute-start(f32[1,32,128]{2,1,0:T(8,128)S(1)} %get-tuple-element.68), channel_id=1, source_target_pairs={{0,32},{32,64},{64,96},{1,33},{33,65},{65,97},{2,34},{34,66},{66,9... | collective-permute-start | bytes 49160 | tf_op jit(solution)/shard_map/ppermute | solution.py:15
  6.0 16.3 %collective-permute-start = (f32[1,32,128]{2,1,0:T(8,128)S(1)}, f32[1,32,128]{2,1,0:T(8,128)S(1)}, u32[]{:S(2)}, u32[]{:S(2)}) collective-permute-start(f32[1,32,128]{2,1,0:T(8,128)S(1)} %get-tuple-element.67), channel_id=1, source_target_pairs={{32,0},{64,32},{96,64},{33,1},{65,33},{97,65},{34,2},{66,34},{98,6... | collective-permute-start | bytes 49160 | tf_op jit(solution)/shard_map/ppermute | solution.py:17
  14.7 24.9 %copy-start.7 = (f32[6,32,32,128]{3,2,1,0:T(8,128)S(1)}, f32[6,32,32,128]{3,2,1,0:T(8,128)}, u32[]{:S(2)}) copy-start(f32[6,32,32,128]{3,2,1,0:T(8,128)} %param.2) | copy-start | bytes 9437188
  15.4 24.2 %collective-permute-start.3 = (f32[6,1,32,128]{3,0,2,1:T(8,128)}, f32[6,1,32,128]{3,0,2,1:T(8,128)S(1)}, u32[]{:S(2)}, u32[]{:S(2)}) collective-permute-start(f32[6,1,32,128]{3,0,2,1:T(8,128)} %get-tuple-element.62), channel_id=1, source_target_pairs={{0,32},{32,64},{64,96},{1,33},{33,65},{65,97},{2,34},{34,66},{66,9... | collective-permute-start | bytes 294920 | tf_op jit(solution)/shard_map/ppermute | solution.py:15
  19.2 23.2 %collective-permute-start.1 = (f32[6,1,32,128]{3,0,2,1:T(8,128)}, f32[6,1,32,128]{3,0,2,1:T(8,128)S(1)}, u32[]{:S(2)}, u32[]{:S(2)}) collective-permute-start(f32[6,1,32,128]{3,0,2,1:T(8,128)} %get-tuple-element.61), channel_id=1, source_target_pairs={{32,0},{64,32},{96,64},{33,1},{65,33},{97,65},{34,2},{66,34},{98,6... | collective-permute-start | bytes 294920 | tf_op jit(solution)/shard_map/ppermute | solution.py:17
  23.5 6.1 %collective-permute-start.4 = (f32[34,1,128]{2,0,1:T(8,128)S(1)}, f32[34,1,128]{2,0,1:T(8,128)S(1)}, u32[]{:S(2)}, u32[]{:S(2)}) collective-permute-start(f32[34,1,128]{2,0,1:T(8,128)S(1)} %copy.172), channel_id=1, source_target_pairs={{8,0},{16,8},{24,16},{9,1},{17,9},{25,17},{10,2},{18,10},{26,18},{... | collective-permute-start | bytes 52232 | tf_op jit(solution)/shard_map/ppermute | solution.py:17
  24.9 5.1 %collective-permute-start.6 = (f32[34,1,128]{2,0,1:T(8,128)S(1)}, f32[34,1,128]{2,0,1:T(8,128)S(1)}, u32[]{:S(2)}, u32[]{:S(2)}) collective-permute-start(f32[34,1,128]{2,0,1:T(8,128)S(1)} %copy.173), channel_id=1, source_target_pairs={{0,8},{8,16},{16,24},{1,9},{9,17},{17,25},{2,10},{10,18},{18,26},{... | collective-permute-start | bytes 52232 | tf_op jit(solution)/shard_map/ppermute | solution.py:15
  32.8 17.9 %collective-permute-start.8 = (f32[34,34,1]{1,0,2:T(8,128)S(1)}, f32[34,34,1]{1,0,2:T(8,128)S(1)}, u32[]{:S(2)}, u32[]{:S(2)}) collective-permute-start(f32[34,34,1]{1,0,2:T(8,128)S(1)} %copy.150), channel_id=1, source_target_pairs={{1,0},{2,1},{3,2},{4,3},{5,4},{6,5},{7,6},{9,8},{10,9},{11,10},{12... | collective-permute-start | bytes 13880 | tf_op jit(solution)/shard_map/ppermute | solution.py:17
  35.6 16.4 %collective-permute-start.10 = (f32[34,34,1]{1,0,2:T(8,128)S(1)}, f32[34,34,1]{1,0,2:T(8,128)S(1)}, u32[]{:S(2)}, u32[]{:S(2)}) collective-permute-start(f32[34,34,1]{1,0,2:T(8,128)S(1)} %copy.154), channel_id=1, source_target_pairs={{0,1},{1,2},{2,3},{3,4},{4,5},{5,6},{6,7},{8,9},{9,10},{10,11},{11... | collective-permute-start | bytes 13880 | tf_op jit(solution)/shard_map/ppermute | solution.py:15
  44.6 8.6 %collective-permute-start.5 = (f32[6,34,1,128]{3,0,2,1:T(8,128)S(1)}, f32[6,34,1,128]{3,0,2,1:T(8,128)S(1)}, u32[]{:S(2)}, u32[]{:S(2)}) collective-permute-start(f32[6,34,1,128]{3,0,2,1:T(8,128)S(1)} %get-tuple-element.56), channel_id=1, source_target_pairs={{8,0},{16,8},{24,16},{9,1},{17,9},{25,17},{10,2},{18,10},{26,18},{... | collective-permute-start | bytes 313352 | tf_op jit(solution)/shard_map/ppermute | solution.py:17
  45.9 7.4 %collective-permute-start.7 = (f32[6,34,1,128]{3,0,2,1:T(8,128)S(1)}, f32[6,34,1,128]{3,0,2,1:T(8,128)S(1)}, u32[]{:S(2)}, u32[]{:S(2)}) collective-permute-start(f32[6,34,1,128]{3,0,2,1:T(8,128)S(1)} %get-tuple-element.55), channel_id=1, source_target_pairs={{0,8},{8,16},{16,24},{1,9},{9,17},{17,25},{2,10},{10,18},{18,26},{... | collective-permute-start | bytes 313352 | tf_op jit(solution)/shard_map/ppermute | solution.py:15
  65.2 14.7 %collective-permute-start.9 = (f32[6,34,34,1]{2,3,1,0:T(1,128)}, f32[6,34,34,1]{2,3,1,0:T(1,128)}, u32[]{:S(2)}, u32[]{:S(2)}) collective-permute-start(f32[6,34,34,1]{2,3,1,0:T(1,128)} %copy.152), channel_id=1, source_target_pairs={{1,0},{2,1},{3,2},{4,3},{5,4},{6,5},{7,6},{9,8},{10,9},{11,10},{12... | collective-permute-start | bytes 83240 | tf_op jit(solution)/shard_map/ppermute | solution.py:17
  70.4 13.9 %collective-permute-start.11 = (f32[6,34,34,1]{2,3,1,0:T(1,128)}, f32[6,34,34,1]{2,3,1,0:T(1,128)}, u32[]{:S(2)}, u32[]{:S(2)}) collective-permute-start(f32[6,34,34,1]{2,3,1,0:T(1,128)} %copy.156), channel_id=1, source_target_pairs={{0,1},{1,2},{2,3},{3,4},{4,5},{5,6},{6,7},{8,9},{9,10},{10,11},{11... | collective-permute-start | bytes 83240 | tf_op jit(solution)/shard_map/ppermute | solution.py:15
  79.9 71.1 %copy-start.8 = (f32[32,32,128]{2,1,0:T(8,128)}, f32[32,32,128]{2,1,0:T(8,128)S(1)}, u32[]{:S(2)}) copy-start(f32[32,32,128]{2,1,0:T(8,128)S(1)} %get-tuple-element.43) | copy-start | bytes 1572868
  104.5 8.8 %collective-permute-start.12 = (f32[6,1,32,128]{3,0,2,1:T(8,128)S(1)}, f32[6,1,32,128]{3,0,2,1:T(8,128)S(1)}, u32[]{:S(2)}, u32[]{:S(2)}) collective-permute-start(f32[6,1,32,128]{3,0,2,1:T(8,128)S(1)} %get-tuple-element.60), channel_id=1, source_target_pairs={{32,0},{64,32},{96,64},{33,1},{65,33},{97,65},{34,2},{66,34},{98,6... | collective-permute-start | bytes 294920 | tf_op jit(solution)/shard_map/ppermute | solution.py:17
  107.7 6.8 %collective-permute-start.13 = (f32[6,1,32,128]{3,0,2,1:T(8,128)S(1)}, f32[6,1,32,128]{3,0,2,1:T(8,128)S(1)}, u32[]{:S(2)}, u32[]{:S(2)}) collective-permute-start(f32[6,1,32,128]{3,0,2,1:T(8,128)S(1)} %get-tuple-element.59), channel_id=1, source_target_pairs={{0,32},{32,64},{64,96},{1,33},{33,65},{65,97},{2,34},{34,66},{66,9... | collective-permute-start | bytes 294920 | tf_op jit(solution)/shard_map/ppermute | solution.py:15
  114.5 6.1 %collective-permute-start.14 = (f32[6,34,1,128]{3,0,2,1:T(8,128)S(1)}, f32[6,34,1,128]{3,0,2,1:T(8,128)S(1)}, u32[]{:S(2)}, u32[]{:S(2)}) collective-permute-start(f32[6,34,1,128]{3,0,2,1:T(8,128)S(1)} %get-tuple-element.54), channel_id=1, source_target_pairs={{8,0},{16,8},{24,16},{9,1},{17,9},{25,17},{10,2},{18,10},{26,18},{... | collective-permute-start | bytes 313352 | tf_op jit(solution)/shard_map/ppermute | solution.py:17
  115.8 6.3 %collective-permute-start.15 = (f32[6,34,1,128]{3,0,2,1:T(8,128)S(1)}, f32[6,34,1,128]{3,0,2,1:T(8,128)S(1)}, u32[]{:S(2)}, u32[]{:S(2)}) collective-permute-start(f32[6,34,1,128]{3,0,2,1:T(8,128)S(1)} %get-tuple-element.53), channel_id=1, source_target_pairs={{0,8},{8,16},{16,24},{1,9},{9,17},{17,25},{2,10},{10,18},{18,26},{... | collective-permute-start | bytes 313352 | tf_op jit(solution)/shard_map/ppermute | solution.py:15
  131.7 10.6 %collective-permute-start.16 = (f32[6,34,34,1]{2,3,1,0:T(1,128)S(1)}, f32[6,34,34,1]{2,3,1,0:T(1,128)}, u32[]{:S(2)}, u32[]{:S(2)}) collective-permute-start(f32[6,34,34,1]{2,3,1,0:T(1,128)S(1)} %copy.158), channel_id=1, source_target_pairs={{1,0},{2,1},{3,2},{4,3},{5,4},{6,5},{7,6},{9,8},{10,9},{11,10},{12... | collective-permute-start | bytes 83240 | tf_op jit(solution)/shard_map/ppermute | solution.py:17
  136.9 9.7 %collective-permute-start.17 = (f32[6,34,34,1]{2,3,1,0:T(1,128)}, f32[6,34,34,1]{2,3,1,0:T(1,128)}, u32[]{:S(2)}, u32[]{:S(2)}) collective-permute-start(f32[6,34,34,1]{2,3,1,0:T(1,128)} %copy.160), channel_id=1, source_target_pairs={{0,1},{1,2},{2,3},{3,4},{4,5},{5,6},{6,7},{8,9},{9,10},{10,11},{11... | collective-permute-start | bytes 83240 | tf_op jit(solution)/shard_map/ppermute | solution.py:15
  169.5 17.7 %copy-start.3 = (f32[6,32,32,128]{3,0,2,1:T(8,128)}, f32[6,32,32,128]{3,0,2,1:T(8,128)S(1)}, u32[]{:S(2)}) copy-start(f32[6,32,32,128]{3,0,2,1:T(8,128)S(1)} %fusion.18) | copy-start | bytes 9437188
  169.5 8.4 %collective-permute-start.18 = (f32[6,1,32,128]{3,0,2,1:T(8,128)S(1)}, f32[6,1,32,128]{3,0,2,1:T(8,128)S(1)}, u32[]{:S(2)}, u32[]{:S(2)}) collective-permute-start(f32[6,1,32,128]{3,0,2,1:T(8,128)S(1)} %get-tuple-element.58), channel_id=1, source_target_pairs={{32,0},{64,32},{96,64},{33,1},{65,33},{97,65},{34,2},{66,34},{98,6... | collective-permute-start | bytes 294920 | tf_op jit(solution)/shard_map/ppermute | solution.py:17
  171.4 7.7 %collective-permute-start.19 = (f32[6,1,32,128]{3,0,2,1:T(8,128)S(1)}, f32[6,1,32,128]{3,0,2,1:T(8,128)S(1)}, u32[]{:S(2)}, u32[]{:S(2)}) collective-permute-start(f32[6,1,32,128]{3,0,2,1:T(8,128)S(1)} %get-tuple-element.57), channel_id=1, source_target_pairs={{0,32},{32,64},{64,96},{1,33},{33,65},{65,97},{2,34},{34,66},{66,9... | collective-permute-start | bytes 294920 | tf_op jit(solution)/shard_map/ppermute | solution.py:15
  179.2 6.6 %collective-permute-start.20 = (f32[6,34,1,128]{3,0,2,1:T(8,128)S(1)}, f32[6,34,1,128]{3,0,2,1:T(8,128)S(1)}, u32[]{:S(2)}, u32[]{:S(2)}) collective-permute-start(f32[6,34,1,128]{3,0,2,1:T(8,128)S(1)} %get-tuple-element.52), channel_id=1, source_target_pairs={{8,0},{16,8},{24,16},{9,1},{17,9},{25,17},{10,2},{18,10},{26,18},{... | collective-permute-start | bytes 313352 | tf_op jit(solution)/shard_map/ppermute | solution.py:17
  180.5 6.7 %collective-permute-start.21 = (f32[6,34,1,128]{3,0,2,1:T(8,128)S(1)}, f32[6,34,1,128]{3,0,2,1:T(8,128)S(1)}, u32[]{:S(2)}, u32[]{:S(2)}) collective-permute-start(f32[6,34,1,128]{3,0,2,1:T(8,128)S(1)} %get-tuple-element.51), channel_id=1, source_target_pairs={{0,8},{8,16},{16,24},{1,9},{9,17},{17,25},{2,10},{10,18},{18,26},{... | collective-permute-start | bytes 313352 | tf_op jit(solution)/shard_map/ppermute | solution.py:15
  196.8 10.0 %collective-permute-start.22 = (f32[6,34,34,1]{2,3,1,0:T(1,128)S(1)}, f32[6,34,34,1]{2,3,1,0:T(1,128)S(1)}, u32[]{:S(2)}, u32[]{:S(2)}) collective-permute-start(f32[6,34,34,1]{2,3,1,0:T(1,128)S(1)} %copy.162), channel_id=1, source_target_pairs={{1,0},{2,1},{3,2},{4,3},{5,4},{6,5},{7,6},{9,8},{10,9},{11,10},{12... | collective-permute-start | bytes 83240 | tf_op jit(solution)/shard_map/ppermute | solution.py:17
  201.4 9.0 %collective-permute-start.23 = (f32[6,34,34,1]{2,3,1,0:T(1,128)S(1)}, f32[6,34,34,1]{2,3,1,0:T(1,128)S(1)}, u32[]{:S(2)}, u32[]{:S(2)}) collective-permute-start(f32[6,34,34,1]{2,3,1,0:T(1,128)S(1)} %copy.164), channel_id=1, source_target_pairs={{0,1},{1,2},{2,3},{3,4},{4,5},{5,6},{6,7},{8,9},{9,10},{10,11},{11... | collective-permute-start | bytes 83240 | tf_op jit(solution)/shard_map/ppermute | solution.py:15
  213.9 19.3 %copy-start.2 = (f32[6,32,32,128]{3,0,2,1:T(8,128)S(1)}, f32[6,32,32,128]{3,0,2,1:T(8,128)}, u32[]{:S(2)}) copy-start(f32[6,32,32,128]{3,0,2,1:T(8,128)} %copy-done.1) | copy-start | bytes 9437188
  213.9 19.3 %copy-start.4 = (f32[6,32,32,128]{3,0,2,1:T(8,128)S(1)}, f32[6,32,32,128]{3,0,2,1:T(8,128)}, u32[]{:S(2)}) copy-start(f32[6,32,32,128]{3,0,2,1:T(8,128)} %copy-done.3) | copy-start | bytes 9437188
  244.2 107.1 %copy-start.19 = (f32[24]{0:T(128)S(1)}, f32[24]{0:T(128)}, u32[]{:S(2)}) copy-start(f32[24]{0:T(128)} %get-tuple-element.100) | copy-start | bytes 292
  244.2 108.7 %copy-start.20 = (f32[24]{0:T(128)S(1)}, f32[24]{0:T(128)}, u32[]{:S(2)}) copy-start(f32[24]{0:T(128)} %get-tuple-element.99) | copy-start | bytes 292
  244.2 110.2 %copy-start.21 = (f32[24]{0:T(128)S(1)}, f32[24]{0:T(128)}, u32[]{:S(2)}) copy-start(f32[24]{0:T(128)} %compare_convert_fusion.15) | copy-start | bytes 292
  244.3 111.8 %copy-start.22 = (f32[24]{0:T(128)S(1)}, f32[24]{0:T(128)}, u32[]{:S(2)}) copy-start(f32[24]{0:T(128)} %get-tuple-element.102) | copy-start | bytes 292
  244.3 113.4 %copy-start.23 = (f32[24]{0:T(128)S(1)}, f32[24]{0:T(128)}, u32[]{:S(2)}) copy-start(f32[24]{0:T(128)} %get-tuple-element.101) | copy-start | bytes 292
  244.3 115.0 %copy-start.28 = (f32[24]{0:T(128)S(1)}, f32[24]{0:T(128)}, u32[]{:S(2)}) copy-start(f32[24]{0:T(128)} %compare_convert_fusion.12) | copy-start | bytes 292
  244.3 116.6 %copy-start.29 = (f32[24]{0:T(128)S(1)}, f32[24]{0:T(128)}, u32[]{:S(2)}) copy-start(f32[24]{0:T(128)} %get-tuple-element.104) | copy-start | bytes 292
  244.3 118.2 %copy-start.30 = (f32[24]{0:T(128)S(1)}, f32[24]{0:T(128)}, u32[]{:S(2)}) copy-start(f32[24]{0:T(128)} %get-tuple-element.103) | copy-start | bytes 292
  244.3 119.8 %copy-start.31 = (f32[24]{0:T(128)S(1)}, f32[24]{0:T(128)}, u32[]{:S(2)}) copy-start(f32[24]{0:T(128)} %get-tuple-element.106) | copy-start | bytes 292
  244.3 121.5 %copy-start.32 = (f32[24]{0:T(128)S(1)}, f32[24]{0:T(128)}, u32[]{:S(2)}) copy-start(f32[24]{0:T(128)} %get-tuple-element.105) | copy-start | bytes 292
  244.3 123.1 %copy-start.37 = (f32[24]{0:T(128)S(1)}, f32[24]{0:T(128)}, u32[]{:S(2)}) copy-start(f32[24]{0:T(128)} %get-tuple-element.108) | copy-start | bytes 292
  244.3 124.8 %copy-start.38 = (f32[24]{0:T(128)S(1)}, f32[24]{0:T(128)}, u32[]{:S(2)}) copy-start(f32[24]{0:T(128)} %get-tuple-element.107) | copy-start | bytes 292
  244.3 126.5 %copy-start.39 = (f32[24]{0:T(128)S(1)}, f32[24]{0:T(128)}, u32[]{:S(2)}) copy-start(f32[24]{0:T(128)} %get-tuple-element.110) | copy-start | bytes 292
  244.3 128.2 %copy-start.40 = (f32[24]{0:T(128)S(1)}, f32[24]{0:T(128)}, u32[]{:S(2)}) copy-start(f32[24]{0:T(128)} %get-tuple-element.109) | copy-start | bytes 292
  244.4 129.8 %copy-start.41 = (f32[24]{0:T(128)S(1)}, f32[24]{0:T(128)}, u32[]{:S(2)}) copy-start(f32[24]{0:T(128)} %get-tuple-element.112) | copy-start | bytes 292
  244.4 131.4 %copy-start.42 = (f32[24]{0:T(128)S(1)}, f32[24]{0:T(128)}, u32[]{:S(2)}) copy-start(f32[24]{0:T(128)} %get-tuple-element.111) | copy-start | bytes 292
  244.4 133.0 %copy-start.43 = (f32[24]{0:T(128)S(1)}, f32[24]{0:T(128)}, u32[]{:S(2)}) copy-start(f32[24]{0:T(128)} %get-tuple-element.114) | copy-start | bytes 292
  244.4 134.7 %copy-start.44 = (f32[24]{0:T(128)S(1)}, f32[24]{0:T(128)}, u32[]{:S(2)}) copy-start(f32[24]{0:T(128)} %get-tuple-element.113) | copy-start | bytes 292
  (21 other events, 155.3 us)
where the time goes:
time: 487 us; the launch traced here: 478 us
  local copies, waits for them, and re-layouts  157 us (32%)
  blocking collectives  83.5 us (17%)
  other arithmetic  78 us (16%)
  starting transfers between devices  74.1 us (15%)
  matrix products  60.5 us (12%)
  between operations  18.3 us (4%)
  waiting for transfers between devices  6 us (1%)
    psum x1, blocking collectives, on_device(): total_gram = lax.psum(gram, ('gx', 'gy', 'gz'))  83.5 us
    unnamed x100, local copies, waits for them, and re-layouts  58.9 us
    ppermute x12, starting transfers between devices, extended(): lax.ppermute(tail, axis, [(i, (i + 1) % count) for i in range(ends)])  54.8 us
    div x3, other arithmetic, stencil(): return 2.5 * accum / diagonal  53.5 us
    slice x9, local copies, waits for them, and re-layouts, extended(): head = lax.slice_in_dim(cells, 0, width, axis=dim)  29.1 us
    dot_general x1, matrix products, on_device(): solved = jnp.dot(inverse, flat, precision=lax.Precision.HIGHEST)  24.5 us
    dot_general x24, matrix products, lower_inverse(): jnp.dot(lower[row_index], inverse, precision=lax.Precision.HIGHEST)  19.6 us
    ppermute x12, starting transfers between devices, extended(): lax.ppermute(head, axis, [((i + 1) % count, i) for i in range(ends)])  19.3 us
  transfers between devices with their start and end apart: 24, of which 8 were waited for; matrix products, arithmetic and copies ran while one was open for 10% of the time, Pallas kernels for 0%

commit v1 on v0

--- a/solution.py
+++ b/solution.py
@@ -99,7 +99,7 @@
     flat = basis.reshape(columns, -1)
     cell_count = flat.shape[1] * lax.axis_size("gx") * lax.axis_size("gy") * lax.axis_size("gz")
     gram = jnp.dot(flat, flat.T, precision=lax.Precision.HIGHEST)
-    total_gram = lax.psum(gram, ("gx", "gy", "gz"))
+    total_gram = jnp.sum(lax.all_gather(gram, ("gx", "gy", "gz")), axis=0)
     factor_r = lower_factor(total_gram / cell_count).T
     inverse = lower_inverse(factor_r.T)
     solved = jnp.dot(inverse, flat, precision=lax.Precision.HIGHEST)

time: 487 us -> 743 us (1.53)
  the two profiles are of different devices: /device:TPU:1 before, /device:TPU:9 now
where the time goes in v1:
time: 743 us; the launch traced here: 734 us
  blocking collectives  346 us (47%)
  local copies, waits for them, and re-layouts  153 us (21%)
  other arithmetic  78.4 us (11%)
  starting transfers between devices  72.1 us (10%)
  matrix products  60.9 us (8%)
  between operations  17.9 us (2%)
    all_gather x1, blocking collectives, on_device(): total_gram = jnp.sum(lax.all_gather(gram, ('gx', 'gy', 'gz')), axis=0)  346 us
    div x3, other arithmetic, stencil(): return 2.5 * accum / diagonal  54.5 us
    unnamed x100, local copies, waits for them, and re-layouts  54.1 us
    ppermute x12, starting transfers between devices, extended(): lax.ppermute(tail, axis, [(i, (i + 1) % count) for i in range(ends)])  41.6 us
    ppermute x12, starting transfers between devices, extended(): lax.ppermute(head, axis, [((i + 1) % count, i) for i in range(ends)])  30.5 us
    slice x9, local copies, waits for them, and re-layouts, extended(): head = lax.slice_in_dim(cells, 0, width, axis=dim)  29.1 us
    dot_general x1, matrix products, on_device(): solved = jnp.dot(inverse, flat, precision=lax.Precision.HIGHEST)  24.8 us
    dot_general x24, matrix products, lower_inverse(): jnp.dot(lower[row_index], inverse, precision=lax.Precision.HIGHEST)  19.6 us
  transfers between devices with their start and end apart: 24, of which 5 were waited for; matrix products, arithmetic and copies ran while one was open for 7% of the time, Pallas kernels for 0%

profile of v1, /device:TPU:9, one launch (start us, length us, event | category | flops | bytes accessed | tf_op | source)
XLA Modules:
  0.0 733.7 jit_solution(10803930602207952580)
XLA Ops:
  2.7 3.2 collective-permute-start
  5.9 4.7 copy.206
  10.6 2.1 copy-done.5
  14.8 4.3 collective-permute-start.1
  22.3 4.2 collective-permute-start.6
  28.7 1.5 copy.190
  31.5 1.5 copy.194
  33.0 4.0 collective-permute-start.10
  37.0 2.8 copy_dynamic-update-slice_fusion
  39.9 2.1 copy-done.6
  43.3 4.3 collective-permute-start.7
  50.6 2.7 pad_maximum_fusion.1
  53.3 5.2 fusion.259
  58.5 3.9 copy.192
  63.8 3.9 copy.196
  67.7 5.1 collective-permute-start.11
  72.8 4.7 compare_select_fusion
  77.5 4.4 copy.193
  82.0 4.3 copy.197
  86.3 15.7 %fusion.31 = f32[6,32,32,128]{3,0,2,1:T(8,128)S(1)} fusion(f32[6,34,34,1]{3,0,2,1:T(8,128)} %copy.197, f32[6,34,1,128]{3,0,2,1:T(8,128)S(1)} %collective-permute-done.5, f32[6,34,32,128]{3,0,2,1:T(8,128)} %copy-done.6, f32[6,34,1,128]{3,0,2,1:T(8,128)S(1)} %collective-permute-done.7, f32[6,34,34,1]{3,0,2,1:T(8,128)} %copy.193, ...), kind=kLoop, calls=%fused_computation.73 | loop fusion | flops 18087936 | bytes 13764800 | tf_op jit(solution)/shard_map/div | solution.py:58
  102.1 6.3 collective-permute-start.12
  110.2 1.4 collective-permute-done.13
  112.9 4.3 collective-permute-start.15
  117.7 1.5 collective-permute-done.15
  120.3 5.2 fusion.258
  125.5 3.3 copy.198
  130.1 3.9 copy.200
  134.0 4.8 collective-permute-start.17
  139.4 4.3 copy.199
  143.7 4.3 copy.201
  148.0 18.7 %fusion.18 = f32[6,32,32,128]{3,0,2,1:T(8,128)S(1)} fusion(f32[6,34,34,1]{3,0,2,1:T(8,128)} %copy.201, f32[6,34,1,128]{3,0,2,1:T(8,128)} %copy-done.15, f32[6,34,1,128]{3,0,2,1:T(8,128)} %copy-done.16, f32[6,1,32,128]{3,0,2,1:T(8,128)S(1)} %collective-permute-done.12, f32[6,32,32,128]{3,0,2,1:T(8,128)} %copy-done.1, ...), kind=kLoop, calls=%fused_computation.42 | loop fusion | flops 24379392 | bytes 10422464 | tf_op jit(solution)/shard_map/div | solution.py:58
  166.8 6.4 collective-permute-start.18
  177.7 4.7 collective-permute-start.21
  185.6 5.2 fusion.257
  190.8 3.3 copy.202
  195.4 3.3 copy.204
  198.7 5.0 collective-permute-start.23
  204.3 3.6 copy.203
  207.8 3.5 copy.205
  211.4 20.1 %fusion.5 = f32[6,32,32,128]{3,0,2,1:T(8,128)} fusion(f32[6,34,34,1]{3,0,2,1:T(8,128)} %copy.205, f32[6,34,1,128]{3,0,2,1:T(8,128)} %copy-done.13, f32[6,34,1,128]{3,0,2,1:T(8,128)} %copy-done.14, f32[6,1,32,128]{3,0,2,1:T(8,128)} %copy-done.11, f32[6,32,32,128]{3,0,2,1:T(8,128)} %copy-done.3, f32[6,1,32,128]{3,0,2,1:T(8,128)} %copy-done.12, ...), kind=kLoop, calls=%fused_computation.11 | loop fusion | flops 24379392 | bytes 10422464 | tf_op jit(solution)/shard_map/div | solution.py:58
  231.5 6.2 pad_maximum_fusion
  237.8 13.1 %convolution_bitcast_fusion = f32[24,24]{1,0:T(8,128)S(1)} fusion(f32[24,32,32,128]{3,0,2,1:T(8,128)S(1)} %pad_maximum_fusion), kind=kOutput, calls=%fused_computation.99 | convolution fusion | flops 905969664 | bytes 12585216 | tf_op jit(solution)/shard_map/dot_general | solution.py:101
  251.0 345.6 %all-gather = f32[3072,24]{1,0:T(8,128)S(1)} all-gather(f32[24,24]{1,0:T(8,128)S(1)} %convolution_bitcast_fusion), channel_id=2, replica_groups=mesh['gx'=4,'gy'=4,'gz'=8] {'gx','gy','gz'}, dimensions={0}, use_global_device_ids=true | all-gather | bytes 297216 | tf_op jit(solution)/shard_map/all_gather | solution.py:102
  637.0 11.5 %copy.207 = f32[24,32,32,128]{3,2,1,0:T(8,128)} copy(f32[24,32,32,128]{3,0,2,1:T(8,128)} %copy-done) | data formatting | bytes 25165824 | tf_op jit(solution)/shard_map/concatenate | solution.py:97
  665.3 16.8 %copy.220 = f32[3,8,1024,128]{3,1,2,0:T(8,128)} copy(f32[3,8,1024,128]{3,2,1,0:T(8,128)} %bitcast.526) | data formatting | bytes 25165824
  682.2 11.3 %copy.215 = f32[3,8,1024,128]{3,2,1,0:T(8,128)} copy(f32[3,8,1024,128]{3,1,2,0:T(8,128)} %copy.220) | data formatting | bytes 25165824
  696.7 24.8 %fusion = f32[24,32,32,128]{3,0,2,1:T(8,128)} fusion(f32[32,32,128,24]{2,1,0,3:T(8,128)} %bitcast.527, f32[24,24]{1,0:T(8,128)S(1)} %multiply_add_fusion.5, f32[24]{0:T(128)S(1)} %fusion.112, f32[24]{0:T(128)S(1)} %copy-done.44, f32[24]{0:T(128)S(1)} %fusion.111, f32[24]{0:T(128)S(1)} %copy-done.43, f32[24]{0:T(128)S(1)} %fusion.110, f32[24]{0:T(128)S(1)} %copy-done.42, ...), kind=kOutput, calls=%fused_computation.2 | convolution fusion | flops 905974272 | bytes 25168896 | tf_op jit(solution)/shard_map/dot_general | solution.py:105
  721.5 11.8 %copy.209 = f32[24,32,32,128]{3,2,1,0:T(8,128)} copy(f32[24,32,32,128]{3,0,2,1:T(8,128)} %fusion) | data formatting | bytes 25165824
  (286 shorter events, 77.3 us)
Async XLA Ops:
  0.6 19.1 %copy-start.10 = (f32[32,32,128]{2,1,0:T(8,128)S(1)}, f32[32,32,128]{2,1,0:T(8,128)}, u32[]{:S(2)}) copy-start(f32[32,32,128]{2,1,0:T(8,128)} %param.3) | copy-start | bytes 1572868
  1.4 18.3 %collective-permute-start.2 = (f32[1,32,128]{2,1,0:T(8,128)S(1)}, f32[1,32,128]{2,1,0:T(8,128)S(1)}, u32[]{:S(2)}, u32[]{:S(2)}) collective-permute-start(f32[1,32,128]{2,1,0:T(8,128)S(1)} %get-tuple-element.70), channel_id=1, source_target_pairs={{0,32},{32,64},{64,96},{1,33},{33,65},{65,97},{2,34},{34,66},{66,9... | collective-permute-start | bytes 49160 | tf_op jit(solution)/shard_map/ppermute | solution.py:15
  2.7 17.0 %collective-permute-start = (f32[1,32,128]{2,1,0:T(8,128)S(1)}, f32[1,32,128]{2,1,0:T(8,128)S(1)}, u32[]{:S(2)}, u32[]{:S(2)}) collective-permute-start(f32[1,32,128]{2,1,0:T(8,128)S(1)} %get-tuple-element.69), channel_id=1, source_target_pairs={{32,0},{64,32},{96,64},{33,1},{65,33},{97,65},{34,2},{66,34},{98,6... | collective-permute-start | bytes 49160 | tf_op jit(solution)/shard_map/ppermute | solution.py:17
  12.7 24.3 %copy-start.7 = (f32[6,32,32,128]{3,2,1,0:T(8,128)S(1)}, f32[6,32,32,128]{3,2,1,0:T(8,128)}, u32[]{:S(2)}) copy-start(f32[6,32,32,128]{3,2,1,0:T(8,128)} %param.2) | copy-start | bytes 9437188
  13.4 23.6 %collective-permute-start.3 = (f32[6,1,32,128]{3,0,2,1:T(8,128)}, f32[6,1,32,128]{3,0,2,1:T(8,128)S(1)}, u32[]{:S(2)}, u32[]{:S(2)}) collective-permute-start(f32[6,1,32,128]{3,0,2,1:T(8,128)} %get-tuple-element.64), channel_id=1, source_target_pairs={{0,32},{32,64},{64,96},{1,33},{33,65},{65,97},{2,34},{34,66},{66,9... | collective-permute-start | bytes 294920 | tf_op jit(solution)/shard_map/ppermute | solution.py:15
  14.8 25.0 %collective-permute-start.1 = (f32[6,1,32,128]{3,0,2,1:T(8,128)}, f32[6,1,32,128]{3,0,2,1:T(8,128)S(1)}, u32[]{:S(2)}, u32[]{:S(2)}) collective-permute-start(f32[6,1,32,128]{3,0,2,1:T(8,128)} %get-tuple-element.63), channel_id=1, source_target_pairs={{32,0},{64,32},{96,64},{33,1},{65,33},{97,65},{34,2},{66,34},{98,6... | collective-permute-start | bytes 294920 | tf_op jit(solution)/shard_map/ppermute | solution.py:17
  20.9 6.0 collective-permute-start.4
  22.3 5.1 collective-permute-start.6
  30.2 17.9 %collective-permute-start.8 = (f32[34,34,1]{1,0,2:T(8,128)S(1)}, f32[34,34,1]{1,0,2:T(8,128)S(1)}, u32[]{:S(2)}, u32[]{:S(2)}) collective-permute-start(f32[34,34,1]{1,0,2:T(8,128)S(1)} %copy.190), channel_id=1, source_target_pairs={{1,0},{2,1},{3,2},{4,3},{5,4},{6,5},{7,6},{9,8},{10,9},{11,10},{12... | collective-permute-start | bytes 13880 | tf_op jit(solution)/shard_map/ppermute | solution.py:17
  33.0 16.4 %collective-permute-start.10 = (f32[34,34,1]{1,0,2:T(8,128)S(1)}, f32[34,34,1]{1,0,2:T(8,128)S(1)}, u32[]{:S(2)}, u32[]{:S(2)}) collective-permute-start(f32[34,34,1]{1,0,2:T(8,128)S(1)} %copy.194), channel_id=1, source_target_pairs={{0,1},{1,2},{2,3},{3,4},{4,5},{5,6},{6,7},{8,9},{9,10},{10,11},{11... | collective-permute-start | bytes 13880 | tf_op jit(solution)/shard_map/ppermute | solution.py:15
  42.0 8.6 %collective-permute-start.5 = (f32[6,34,1,128]{3,0,2,1:T(8,128)S(1)}, f32[6,34,1,128]{3,0,2,1:T(8,128)S(1)}, u32[]{:S(2)}, u32[]{:S(2)}) collective-permute-start(f32[6,34,1,128]{3,0,2,1:T(8,128)S(1)} %get-tuple-element.58), channel_id=1, source_target_pairs={{8,0},{16,8},{24,16},{9,1},{17,9},{25,17},{10,2},{18,10},{26,18},{... | collective-permute-start | bytes 313352 | tf_op jit(solution)/shard_map/ppermute | solution.py:17
  43.3 7.3 collective-permute-start.7
  62.5 15.1 %collective-permute-start.9 = (f32[6,34,34,1]{2,3,1,0:T(1,128)}, f32[6,34,34,1]{2,3,1,0:T(1,128)}, u32[]{:S(2)}, u32[]{:S(2)}) collective-permute-start(f32[6,34,34,1]{2,3,1,0:T(1,128)} %copy.192), channel_id=1, source_target_pairs={{1,0},{2,1},{3,2},{4,3},{5,4},{6,5},{7,6},{9,8},{10,9},{11,10},{12... | collective-permute-start | bytes 83240 | tf_op jit(solution)/shard_map/ppermute | solution.py:17
  67.7 14.3 %collective-permute-start.11 = (f32[6,34,34,1]{2,3,1,0:T(1,128)}, f32[6,34,34,1]{2,3,1,0:T(1,128)}, u32[]{:S(2)}, u32[]{:S(2)}) collective-permute-start(f32[6,34,34,1]{2,3,1,0:T(1,128)} %copy.196), channel_id=1, source_target_pairs={{0,1},{1,2},{2,3},{3,4},{4,5},{5,6},{6,7},{8,9},{9,10},{10,11},{11... | collective-permute-start | bytes 83240 | tf_op jit(solution)/shard_map/ppermute | solution.py:15
  77.5 70.5 %copy-start.8 = (f32[32,32,128]{2,1,0:T(8,128)}, f32[32,32,128]{2,1,0:T(8,128)S(1)}, u32[]{:S(2)}) copy-start(f32[32,32,128]{2,1,0:T(8,128)S(1)} %get-tuple-element.45) | copy-start | bytes 1572868
  102.1 8.1 %collective-permute-start.12 = (f32[6,1,32,128]{3,0,2,1:T(8,128)S(1)}, f32[6,1,32,128]{3,0,2,1:T(8,128)S(1)}, u32[]{:S(2)}, u32[]{:S(2)}) collective-permute-start(f32[6,1,32,128]{3,0,2,1:T(8,128)S(1)} %get-tuple-element.62), channel_id=1, source_target_pairs={{32,0},{64,32},{96,64},{33,1},{65,33},{97,65},{34,2},{66,34},{98,6... | collective-permute-start | bytes 294920 | tf_op jit(solution)/shard_map/ppermute | solution.py:17
  108.3 3.2 collective-permute-start.13
  111.6 6.1 collective-permute-start.14
  112.9 6.3 collective-permute-start.15
  128.8 10.6 %collective-permute-start.16 = (f32[6,34,34,1]{2,3,1,0:T(1,128)S(1)}, f32[6,34,34,1]{2,3,1,0:T(1,128)}, u32[]{:S(2)}, u32[]{:S(2)}) collective-permute-start(f32[6,34,34,1]{2,3,1,0:T(1,128)S(1)} %copy.198), channel_id=1, source_target_pairs={{1,0},{2,1},{3,2},{4,3},{5,4},{6,5},{7,6},{9,8},{10,9},{11,10},{12... | collective-permute-start | bytes 83240 | tf_op jit(solution)/shard_map/ppermute | solution.py:17
  134.0 9.7 %collective-permute-start.17 = (f32[6,34,34,1]{2,3,1,0:T(1,128)}, f32[6,34,34,1]{2,3,1,0:T(1,128)}, u32[]{:S(2)}, u32[]{:S(2)}) collective-permute-start(f32[6,34,34,1]{2,3,1,0:T(1,128)} %copy.200), channel_id=1, source_target_pairs={{0,1},{1,2},{2,3},{3,4},{4,5},{5,6},{6,7},{8,9},{9,10},{10,11},{11... | collective-permute-start | bytes 83240 | tf_op jit(solution)/shard_map/ppermute | solution.py:15
  166.7 17.7 %copy-start.3 = (f32[6,32,32,128]{3,0,2,1:T(8,128)}, f32[6,32,32,128]{3,0,2,1:T(8,128)S(1)}, u32[]{:S(2)}) copy-start(f32[6,32,32,128]{3,0,2,1:T(8,128)S(1)} %fusion.18) | copy-start | bytes 9437188
  166.8 8.2 %collective-permute-start.18 = (f32[6,1,32,128]{3,0,2,1:T(8,128)S(1)}, f32[6,1,32,128]{3,0,2,1:T(8,128)S(1)}, u32[]{:S(2)}, u32[]{:S(2)}) collective-permute-start(f32[6,1,32,128]{3,0,2,1:T(8,128)S(1)} %get-tuple-element.60), channel_id=1, source_target_pairs={{32,0},{64,32},{96,64},{33,1},{65,33},{97,65},{34,2},{66,34},{98,6... | collective-permute-start | bytes 294920 | tf_op jit(solution)/shard_map/ppermute | solution.py:17
  173.1 3.2 collective-permute-start.19
  176.4 6.6 collective-permute-start.20
  177.7 6.7 collective-permute-start.21
  194.1 10.2 %collective-permute-start.22 = (f32[6,34,34,1]{2,3,1,0:T(1,128)S(1)}, f32[6,34,34,1]{2,3,1,0:T(1,128)S(1)}, u32[]{:S(2)}, u32[]{:S(2)}) collective-permute-start(f32[6,34,34,1]{2,3,1,0:T(1,128)S(1)} %copy.202), channel_id=1, source_target_pairs={{1,0},{2,1},{3,2},{4,3},{5,4},{6,5},{7,6},{9,8},{10,9},{11,10},{12... | collective-permute-start | bytes 83240 | tf_op jit(solution)/shard_map/ppermute | solution.py:17
  198.7 9.2 %collective-permute-start.23 = (f32[6,34,34,1]{2,3,1,0:T(1,128)S(1)}, f32[6,34,34,1]{2,3,1,0:T(1,128)S(1)}, u32[]{:S(2)}, u32[]{:S(2)}) collective-permute-start(f32[6,34,34,1]{2,3,1,0:T(1,128)S(1)} %copy.204), channel_id=1, source_target_pairs={{0,1},{1,2},{2,3},{3,4},{4,5},{5,6},{6,7},{8,9},{9,10},{10,11},{11... | collective-permute-start | bytes 83240 | tf_op jit(solution)/shard_map/ppermute | solution.py:15
  211.4 20.1 %copy-start.2 = (f32[6,32,32,128]{3,0,2,1:T(8,128)S(1)}, f32[6,32,32,128]{3,0,2,1:T(8,128)}, u32[]{:S(2)}) copy-start(f32[6,32,32,128]{3,0,2,1:T(8,128)} %copy-done.1) | copy-start | bytes 9437188
  211.4 20.1 %copy-start.4 = (f32[6,32,32,128]{3,0,2,1:T(8,128)S(1)}, f32[6,32,32,128]{3,0,2,1:T(8,128)}, u32[]{:S(2)}) copy-start(f32[6,32,32,128]{3,0,2,1:T(8,128)} %copy-done.3) | copy-start | bytes 9437188
  237.7 369.5 %copy-start.19 = (f32[24]{0:T(128)S(1)}, f32[24]{0:T(128)}, u32[]{:S(2)}) copy-start(f32[24]{0:T(128)} %get-tuple-element.102) | copy-start | bytes 292
  237.7 371.1 %copy-start.20 = (f32[24]{0:T(128)S(1)}, f32[24]{0:T(128)}, u32[]{:S(2)}) copy-start(f32[24]{0:T(128)} %get-tuple-element.101) | copy-start | bytes 292
  237.7 372.7 %copy-start.21 = (f32[24]{0:T(128)S(1)}, f32[24]{0:T(128)}, u32[]{:S(2)}) copy-start(f32[24]{0:T(128)} %get-tuple-element.104) | copy-start | bytes 292
  237.8 374.2 %copy-start.22 = (f32[24]{0:T(128)S(1)}, f32[24]{0:T(128)}, u32[]{:S(2)}) copy-start(f32[24]{0:T(128)} %get-tuple-element.103) | copy-start | bytes 292
  237.8 375.7 %copy-start.23 = (f32[24]{0:T(128)S(1)}, f32[24]{0:T(128)}, u32[]{:S(2)}) copy-start(f32[24]{0:T(128)} %get-tuple-element.106) | copy-start | bytes 292
  237.8 377.3 %copy-start.28 = (f32[24]{0:T(128)S(1)}, f32[24]{0:T(128)}, u32[]{:S(2)}) copy-start(f32[24]{0:T(128)} %get-tuple-element.105) | copy-start | bytes 292
  250.9 365.8 %copy-start.29 = (f32[24]{0:T(128)S(1)}, f32[24]{0:T(128)}, u32[]{:S(2)}) copy-start(f32[24]{0:T(128)} %get-tuple-element.108) | copy-start | bytes 292
  250.9 367.4 %copy-start.30 = (f32[24]{0:T(128)S(1)}, f32[24]{0:T(128)}, u32[]{:S(2)}) copy-start(f32[24]{0:T(128)} %get-tuple-element.107) | copy-start | bytes 292
  250.9 369.0 %copy-start.31 = (f32[24]{0:T(128)S(1)}, f32[24]{0:T(128)}, u32[]{:S(2)}) copy-start(f32[24]{0:T(128)} %get-tuple-element.110) | copy-start | bytes 292
  250.9 370.6 %copy-start.32 = (f32[24]{0:T(128)S(1)}, f32[24]{0:T(128)}, u32[]{:S(2)}) copy-start(f32[24]{0:T(128)} %get-tuple-element.109) | copy-start | bytes 292
  250.9 372.2 %copy-start.37 = (f32[24]{0:T(128)S(1)}, f32[24]{0:T(128)}, u32[]{:S(2)}) copy-start(f32[24]{0:T(128)} %get-tuple-element.112) | copy-start | bytes 292
  250.9 373.8 %copy-start.38 = (f32[24]{0:T(128)S(1)}, f32[24]{0:T(128)}, u32[]{:S(2)}) copy-start(f32[24]{0:T(128)} %get-tuple-element.111) | copy-start | bytes 292
  250.9 375.4 %copy-start.39 = (f32[24]{0:T(128)S(1)}, f32[24]{0:T(128)}, u32[]{:S(2)}) copy-start(f32[24]{0:T(128)} %get-tuple-element.114) | copy-start | bytes 292
  250.9 377.1 %copy-start.40 = (f32[24]{0:T(128)S(1)}, f32[24]{0:T(128)}, u32[]{:S(2)}) copy-start(f32[24]{0:T(128)} %get-tuple-element.113) | copy-start | bytes 292
  250.9 378.7 %copy-start.41 = (f32[24]{0:T(128)S(1)}, f32[24]{0:T(128)}, u32[]{:S(2)}) copy-start(f32[24]{0:T(128)} %get-tuple-element.116) | copy-start | bytes 292
  250.9 380.4 %copy-start.42 = (f32[24]{0:T(128)S(1)}, f32[24]{0:T(128)}, u32[]{:S(2)}) copy-start(f32[24]{0:T(128)} %get-tuple-element.115) | copy-start | bytes 292
  251.0 382.0 %copy-start.43 = (f32[24]{0:T(128)S(1)}, f32[24]{0:T(128)}, u32[]{:S(2)}) copy-start(f32[24]{0:T(128)} %get-tuple-element.118) | copy-start | bytes 292
  251.0 383.7 %copy-start.44 = (f32[24]{0:T(128)S(1)}, f32[24]{0:T(128)}, u32[]{:S(2)}) copy-start(f32[24]{0:T(128)} %get-tuple-element.117) | copy-start | bytes 292
  (21 other events, 164.7 us)
